TPU v7x, 512 devices: a whole 4x8x8 slice. The times are simulated.
512 devices in a mesh: lhs: 32 (over z_hi, y, core), rhs: 16 (over z_lo, x).
Axes of the slice: x: 4, y: 8, z: 8 (z_hi: 2, z_lo: 4; z = z_hi * 4 + z_lo), core: 2. Of those that a mesh axis runs over, the one named last changes fastest.
Arguments:
- left_table: float32 [32, 16, 384, 400], P('lhs', 'rhs'), may hold values from -6 to 6
- left_state: float32 [32, 16, 384], P('lhs', 'rhs'), may hold values from 1e-06 to 0.0001
- right_table: float32 [32, 16, 384, 400], P('lhs', 'rhs'), may hold values from -6 to 6
- right_state: float32 [32, 16, 384], P('lhs', 'rhs'), may hold values from 1e-06 to 0.0001
- operators: float32 [2, 400, 400], replicated, may hold values from -0.3125 to 0.3125
- operator_state: float32 [2, 400], replicated, may hold values from 0.1 to 10
- sources: int32 [32, 16, 384], P('lhs', 'rhs'), may hold values from 0 to 383
- targets: int32 [32, 16, 384], P('lhs', 'rhs'), may hold values from 0 to 383
- relations: int32 [32, 16, 384], P('lhs', 'rhs'), may hold values from 0 to 1, as said below
- negatives: int32 [32, 16, 384], P('lhs', 'rhs'), may hold values from 0 to 383
- counts: int32 [32, 16], P('lhs', 'rhs'), may hold values from 1 to 384, 3840 in all within a row
Outputs:
- new_left: float32 [32, 16, 384, 400], P('lhs', 'rhs')
- new_right: float32 [32, 16, 384, 400], P('lhs', 'rhs')
- new_operators: float32 [2, 400, 400], replicated
Inputs may be any that keep to these rules, and one draw needn't show every extreme that they name: For each index along lhs, the counts over rhs sum to 3840, and at least one of them equals 384. `relations`: within each bucket the edge slots are grouped by relation: relation ids never fall from one slot to the next.
All inputs are finite; a program needn't handle non-finite values. No bound on the sum of `counts` on one device may be relied on, other than what follows from the above.
Results may differ from a plain program's by a relative error of at most 0.0003.
Values sent between devices are 32-bit elements; how exact they have to be, the bound alone decides.
A program may use at most 64 MiB of HBM per device.

v0:
```python
import jax
import jax.numpy as jnp
from jax import lax
from jax.sharding import PartitionSpec as P


def from_behind(value, axis, steps):
    count = lax.axis_size(axis)
    pairs = [(source, (source + steps) % count) for source in range(count)]
    return lax.ppermute(value, axis, pairs)


def map_edges(inputs, operators, relations):
    edge_count, feat_width = inputs.shape
    block_len = min(128, edge_count)
    blocks = edge_count // block_len
    grouped = relations.reshape(blocks, block_len)
    firsts = grouped[:, 0]
    picked = operators[firsts]
    shaped = inputs.reshape(blocks, block_len, feat_width)
    mapped = jnp.einsum("nbw,nwv->nbv", shaped, picked, precision=lax.Precision.HIGHEST)
    split_at = jnp.sum((relations == 0).astype(jnp.int32))
    edge_block = jnp.minimum(split_at // block_len, blocks - 1)
    boundary = lax.dynamic_index_in_dim(shaped, edge_block, 0, keepdims=False)
    patched = jnp.dot(boundary, operators[operators.shape[0] - 1], precision=lax.Precision.HIGHEST)
    block_ids = jnp.arange(blocks, dtype=jnp.int32)
    needs_patch = (block_ids[:, None] == edge_block) & (grouped == 1)
    mapped = jnp.where(needs_patch[:, :, None], patched[None], mapped)
    return mapped.reshape(edge_count, feat_width)


def bucket_loss(
    left_block, right_block, operators, sources, targets, relations, negatives, live_count
):
    inputs = left_block[sources]
    mapped = map_edges(inputs, operators, relations)
    unit_mapped = mapped * lax.rsqrt(jnp.sum(mapped * mapped, -1, keepdims=True) + 1e-06)
    unit_right = right_block * lax.rsqrt(
        jnp.sum(right_block * right_block, -1, keepdims=True) + 1e-06
    )
    positive = jnp.sum(unit_mapped * unit_right[targets], -1)
    sampled = jnp.dot(unit_mapped, unit_right[negatives].T, precision=lax.Precision.HIGHEST)
    log_total = jnp.log(jnp.exp(positive) + jnp.sum(jnp.exp(sampled), -1))
    live_slot = jnp.arange(sources.shape[0], dtype=jnp.int32) < live_count
    return jnp.sum(jnp.where(live_slot, log_total - positive, jnp.zeros_like(log_total)))


def adagrad(weights, sums_in, gradient):
    summed = sums_in + jnp.mean(gradient * gradient, -1)
    return weights - 0.1 * gradient / jnp.sqrt(summed)[..., None]


def body(
    left_table,
    left_state,
    right_table,
    right_state,
    operators,
    operator_state,
    sources,
    targets,
    relations,
    negatives,
    counts,
):
    left_block, left_bstate = from_behind((left_table, left_state), "lhs", 1)
    right_block, right_bstate = from_behind((right_table, right_state), "rhs", 1)

    def local_loss(first, second, third):
        return bucket_loss(
            first,
            second,
            third,
            sources[0, 0],
            targets[0, 0],
            relations[0, 0],
            negatives[0, 0],
            counts[0, 0],
        )

    loss_value, pullback = jax.vjp(local_loss, left_block[0, 0], right_block[0, 0], operators)
    left_grad, right_grad, operator_grad = pullback(jnp.ones_like(loss_value))
    new_left = adagrad(left_block[0, 0], left_bstate[0, 0], left_grad)[None, None]
    new_right = adagrad(right_block[0, 0], right_bstate[0, 0], right_grad)[None, None]
    summed = lax.psum(operator_grad, ("lhs", "rhs"))
    new_operators = adagrad(operators, operator_state, summed)
    return (new_left, new_right, new_operators)


def solution(mesh):
    return jax.shard_map(
        body,
        mesh=mesh,
        in_specs=(
            P("lhs", "rhs", None, None),
            P("lhs", "rhs", None),
            P("lhs", "rhs", None, None),
            P("lhs", "rhs", None),
            P(),
            P(),
            P("lhs", "rhs", None),
            P("lhs", "rhs", None),
            P("lhs", "rhs", None),
            P("lhs", "rhs", None),
            P("lhs", "rhs"),
        ),
        out_specs=(P("lhs", "rhs", None, None), P("lhs", "rhs", None, None), P()),
        check_vma=False,
    )
```

profile of v0, /device:TPU:1, one launch (start us, length us, event | category | flops | bytes accessed | tf_op | source)
XLA Modules:
  0.0 394.6 jit_solution(9089454777289385931)
XLA Ops:
  7.2 4.6 %collective-permute-start.2 = (f32[1,1,384]{2,1,0:T(1,128)}, f32[1,1,384]{2,1,0:T(1,128)S(1)}, u32[]{:S(2)}, u32[]{:S(2)}) collective-permute-start(f32[1,1,384]{2,1,0:T(1,128)} %param.12), channel_id=1, source_target_pairs={{0,16},{16,32},{32,48},{48,64},{64,80},{80,96},{96,112},{112,128},... | collective-permute-start | bytes 4616 | tf_op jit(solution)/shard_map/ppermute | solution.py:10
  11.8 3.1 collective-permute-start.3
  14.9 2.2 collective-permute-start
  17.1 3.1 collective-permute-start.1
  27.2 2.1 gather_fusion.1
  29.4 1.8 copy.41
  31.2 2.2 gather_fusion
  33.5 3.0 fusion.3
  36.5 5.7 %multiply_reduce_fusion.4 = (f32[3,128]{1,0:T(4,128)S(1)}, f32[3,128,400]{1,2,0:T(8,128)}) fusion(f32[3,128,400]{2,1,0:T(8,128)S(1)} %bitcast.119, f32[3,400,400]{2,1,0:T(8,128)S(1)} %gather_fusion.1, f32[128,400]{0,1:T(8,128)S(1)} %fusion.3, pred[3,128]{1,0:T(4,128)(4,1)S(1)} %compare_and_fusion), kind=kOutput, calls=%fused_computation.44 | convolution fusion | flops 737740416 | bytes 3355520 | tf_op jit(solution)/shard_map/jvp(nbw,nwv->nbv)/dot_general | solution.py:21
  42.2 10.4 %collective-permute-done.1 = f32[1,1,384,400]{2,3,1,0:T(8,128)} collective-permute-done((f32[1,1,384,400]{2,3,1,0:T(8,128)}, f32[1,1,384,400]{2,3,1,0:T(8,128)}, u32[]{:S(2)}, u32[]{:S(2)}) %collective-permute-start.1) | collective-permute-done | bytes 614432 | tf_op jit(solution)/shard_map/ppermute | solution.py:10
  52.6 1.3 copy.45
  54.2 1.6 gather_fusion.3
  55.9 2.2 gather_fusion.2
  58.1 2.3 copy.49
  60.4 2.2 copy.47
  63.8 1.5 fusion.51
  65.3 2.3 fusion.15
  67.6 1.6 fusion.11
  69.4 1.5 copy-done.1
  70.9 3.0 fusion.14
  74.0 4.1 %fusion.13 = f32[3,400,400]{2,1,0:T(8,128)} fusion(f32[3,128,400]{2,1,0:T(8,128)S(1)} %bitcast.120, f32[50,3,8,128]{3,2,1,0:T(8,128)S(1)} %get-tuple-element.15, pred[3,128]{1,0:T(4,128)(4,1)S(1)} %compare_and_fusion), kind=kOutput, calls=%fused_computation.45 | convolution fusion | flops 737433600 | bytes 3149184 | tf_op jit(solution)/shard_map/transpose(jvp(nbw,nwv->nbv))/dot_general | solution.py:21
  79.2 3.8 scatter_custom_fusion.1
  83.1 3.6 scatter_custom_fusion.2
  88.4 2.3 copy.58
  90.8 2.8 convolution_bitcast_fusion
  95.6 3.6 scatter_custom_fusion
  99.2 2.5 pad.3
  101.7 7.2 %scatter_fusion = f32[2,400,400]{2,1,0:T(8,128)} fusion(f32[2,400,400]{2,1,0:T(8,128)} %pad.3, s32[3]{0:T(128)S(1)} %fusion.48, f32[3,400,400]{2,1,0:T(8,128)} %fusion.13), kind=kCustom, calls=%fused_computation.7 | custom fusion | flops 480000 | bytes 5760012 | tf_op jit(solution)/shard_map/transpose(jvp())/scatter-add | solution.py:19
  110.2 2.2 copy.57
  112.4 272.0 %all-reduce.3.cloned.1.call-done = f32[2,400,400]{2,1,0:T(8,128)} async-done(((f32[2,400,400]{2,1,0:T(8,128)}), f32[2,400,400]{2,1,0:T(8,128)}) %all-reduce.3.cloned.1.call-update) | async-done | bytes 1280016 | tf_op jit(solution)/shard_map/psum | solution.py:85
  384.3 1.8 multiply_reduce_fusion
  386.2 1.5 divide_subtract_fusion
  (60 shorter events, 11.6 us)
Async XLA Ops:
  7.2 377.2 %all-reduce.3.cloned.1.call-start = ((), (), s32[]{:S(2)}) async-start(), calls=%async_computation | async-start | bytes 3276800 | tf_op jit(solution)/shard_map/psum | solution.py:85
  7.2 22.2 %collective-permute-start.2 = (f32[1,1,384]{2,1,0:T(1,128)}, f32[1,1,384]{2,1,0:T(1,128)S(1)}, u32[]{:S(2)}, u32[]{:S(2)}) collective-permute-start(f32[1,1,384]{2,1,0:T(1,128)} %param.12), channel_id=1, source_target_pairs={{0,16},{16,32},{32,48},{48,64},{64,80},{80,96},{96,112},{112,128},... | collective-permute-start | bytes 4616 | tf_op jit(solution)/shard_map/ppermute | solution.py:10
  11.8 17.6 %collective-permute-start.3 = (f32[1,1,384]{2,1,0:T(1,128)}, f32[1,1,384]{2,1,0:T(1,128)S(1)}, u32[]{:S(2)}, u32[]{:S(2)}) collective-permute-start(f32[1,1,384]{2,1,0:T(1,128)} %param.14), channel_id=1, source_target_pairs={{0,1},{1,2},{2,3},{3,4},{4,5},{5,6},{6,7},{7,8},{8,9},{9,10},{10,1... | collective-permute-start | bytes 4616 | tf_op jit(solution)/shard_map/ppermute | solution.py:10
  14.9 14.5 %collective-permute-start = (f32[1,1,384,400]{2,3,1,0:T(8,128)}, f32[1,1,384,400]{2,3,1,0:T(8,128)}, u32[]{:S(2)}, u32[]{:S(2)}) collective-permute-start(f32[1,1,384,400]{2,3,1,0:T(8,128)} %param.11), channel_id=1, source_target_pairs={{0,16},{16,32},{32,48},{48,64},{64,80},{80,96},{96,112},{112,128},... | collective-permute-start | bytes 1843208 | tf_op jit(solution)/shard_map/ppermute | solution.py:10
  17.1 35.4 %collective-permute-start.1 = (f32[1,1,384,400]{2,3,1,0:T(8,128)}, f32[1,1,384,400]{2,3,1,0:T(8,128)}, u32[]{:S(2)}, u32[]{:S(2)}) collective-permute-start(f32[1,1,384,400]{2,3,1,0:T(8,128)} %param.13), channel_id=1, source_target_pairs={{0,1},{1,2},{2,3},{3,4},{4,5},{5,6},{6,7},{7,8},{8,9},{9,10},{10,1... | collective-permute-start | bytes 1843208 | tf_op jit(solution)/shard_map/ppermute | solution.py:10
  29.4 7.2 %copy-start = (f32[3,400,400]{2,1,0:T(8,128)}, f32[3,400,400]{2,1,0:T(8,128)S(1)}, u32[]{:S(2)}) copy-start(f32[3,400,400]{2,1,0:T(8,128)S(1)} %gather_fusion.1) | copy-start | bytes 5760004
  33.5 3.0 copy-start.4
  58.1 4.5 %copy-start.2 = (f32[3,128,400]{1,2,0:T(8,128)S(1)}, f32[3,128,400]{1,2,0:T(8,128)}, u32[]{:S(2)}) copy-start(f32[3,128,400]{1,2,0:T(8,128)} %get-tuple-element.19) | copy-start | bytes 1843204
  63.8 3.8 copy-start.8
  69.2 1.7 copy-start.1
  70.9 3.1 copy-start.5
  88.4 5.2 %copy-start.3 = (f32[2,400,400]{2,1,0:T(8,128)S(1)}, f32[2,400,400]{2,1,0:T(8,128)}, u32[]{:S(2)}) copy-start(f32[2,400,400]{2,1,0:T(8,128)} %param.15) | copy-start | bytes 3840004
  88.4 5.2 %copy-start.7 = (f32[3,128,400]{1,2,0:T(8,128)S(1)}, f32[3,128,400]{1,2,0:T(8,128)}, u32[]{:S(2)}) copy-start(f32[3,128,400]{1,2,0:T(8,128)} %fusion.14) | copy-start | bytes 1843204
  110.2 276.0 %copy-start.9 = (f32[2,400]{1,0:T(2,128)S(1)}, f32[2,400]{1,0:T(2,128)}, u32[]{:S(2)}) copy-start(f32[2,400]{1,0:T(2,128)} %param.16) | copy-start | bytes 9604
  384.3 1.9 copy-start.6
Sparse Core Ops, SparseCore 0:
  109.0 275.2 all-reduce.2
where the time goes:
time: 396 us; the launch traced here: 395 us
  waiting for transfers between devices  282 us (71%)
  other arithmetic  29.7 us (8%)
  local copies, waits for them, and re-layouts  27 us (7%)
  matrix products  24.9 us (6%)
  between operations  17.6 us (4%)
  starting transfers between devices  13.1 us (3%)
    psum x1, waiting for transfers between devices, body(): summed = lax.psum(operator_grad, ('lhs', 'rhs'))  272 us
    ppermute x4, starting transfers between devices, from_behind(): return lax.ppermute(value, axis, pairs)  13 us
    dot_general x3, matrix products, map_edges(): jnp.einsum('nbw,nwv->nbv', shaped, picked, precision=lax.Precision.HIGHEST)  12.8 us
    ppermute x4, waiting for transfers between devices, from_behind(): return lax.ppermute(value, axis, pairs)  10.4 us
  transfers between devices with their start and end apart: 5, of which 2 were waited for; matrix products, arithmetic and copies ran while one was open for 6% of the time, Pallas kernels for 0%

commit v1 on v0

v1 whole, which is shorter than its diff:
```python
import functools

import jax
import jax.numpy as jnp
from jax import lax
from jax.experimental import pallas as pl
from jax.experimental.pallas import tpu as pltpu
from jax.sharding import PartitionSpec as P

MESH = pl.DeviceIdType.MESH
F32 = jnp.float32
BF16 = jnp.bfloat16

ROWS = 384
WIDTH = 400
LANES = 512
NX, NY, NZ = 4, 8, 8

X0, XC = 0, 48
Y0, YC = 192, 16
Z0, ZC = 320, 16
PADDED = 448

NN = (((1,), (0,)), ((), ()))
NT = (((1,), (1,)), ((), ()))


def split(value):
    high = value.astype(BF16)
    return high, (value - high.astype(F32)).astype(BF16)


def dot(a, b, dims=NN):
    return lax.dot_general(a, b, dims, preferred_element_type=F32)


def dot3(a, b, dims=NN):
    (a_high, a_low), (b_high, b_low) = a, b
    return dot(a_high, b_high, dims) + (dot(a_high, b_low, dims) + dot(a_low, b_high, dims))


def device(x, y, z, c):
    return ((z // 4) * 16 + y * 2 + c, (z % 4) * 4 + x)


def adagrad(weights, sums, gradient):
    summed = sums + jnp.sum(gradient * gradient, -1, keepdims=True) * (1.0 / WIDTH)
    return weights - gradient * (0.1 / jnp.sqrt(summed))


def kernel(
    left_ref, lstate_ref, right_ref, rstate_ref, ops_ref, opstate_ref,
    src_ref, tgt_ref, rel_ref, neg_ref, cnt_ref,
    new_left_ref, new_right_ref, new_ops_ref,
    left, right, lstate, rstate, ops, out_left, out_right, out_ops, rows8, state8,
    grad, sibling, total,
    rx, ry, rz, qx, qy, qz, r2x, r2y, r2z, r3x, r3y, r3z, fx, fy, fz,
    perm_send, perm_recv, local_sem, out_sem,
    core_send, core_recv, s1, v1, s2, v2, s3, v3, s4, v4, s5, v5, s6, v6,
):
    lhs, rhs = lax.axis_index("lhs"), lax.axis_index("rhs")
    mx, my, mz, mc = rhs % 4, (lhs // 2) % 8, (lhs // 16) * 4 + rhs // 4, lhs % 2
    other = 1 - mc

    def along(axis, steps):
        if axis == "x":
            return device((mx + steps) % NX, my, mz, mc)
        if axis == "y":
            return device(mx, (my + steps) % NY, mz, mc)
        return device(mx, my, (mz + steps) % NZ, mc)

    pair = device(mx, my, mz, other)
    lhs_next, lhs_prev = ((lhs + 1) % 32, rhs), ((lhs + 31) % 32, rhs)
    rhs_next, rhs_prev = (lhs, (rhs + 1) % 16), (lhs, (rhs + 15) % 16)
    size = {"x": NX, "y": NY, "z": NZ}
    me = {"x": mx, "y": my, "z": mz}

    ops_copy = pltpu.make_async_copy(ops_ref, ops, local_sem.at[0])
    ops_copy.start()

    peers = [lhs_next, lhs_prev, rhs_next, rhs_prev, pair]
    peers += [along(axis, steps) for axis in "xyz" for steps in range(1, size[axis])]
    barrier = pltpu.get_barrier_semaphore()
    for peer in peers:
        pl.semaphore_signal(barrier, inc=1, device_id=peer, device_id_type=MESH)
    pl.semaphore_wait(barrier, len(peers))

    def send(src, dst, ssem, rsem, target):
        copy = pltpu.make_async_remote_copy(
            src_ref=src, dst_ref=dst, send_sem=ssem, recv_sem=rsem, device_id=target, device_id_type=MESH
        )
        copy.start()
        return copy

    right_copy = send(right_ref, right, perm_send.at[0], perm_recv.at[0], rhs_next)
    left_copy = send(left_ref, left, perm_send.at[1], perm_recv.at[1], lhs_next)
    rstate_copy = send(rstate_ref, rstate, perm_send.at[2], perm_recv.at[2], rhs_next)
    lstate_copy = send(lstate_ref, lstate, perm_send.at[3], perm_recv.at[3], lhs_next)

    grad[...] = jnp.zeros_like(grad)
    rows8[0:1, :] = src_ref[...].astype(F32)
    rows8[1:2, :] = tgt_ref[...].astype(F32)
    rows8[2:3, :] = rel_ref[...].astype(F32)
    rows8[3:4, :] = neg_ref[...].astype(F32)
    rows8[4:8, :] = jnp.zeros((4, ROWS), F32)
    columns = rows8[...].T
    lane = lax.broadcasted_iota(jnp.int32, (ROWS, ROWS), 1).astype(F32)
    sublane = lax.broadcasted_iota(jnp.int32, (ROWS, ROWS), 0).astype(F32)
    hot_src = (columns[:, 0:1] == lane).astype(F32).astype(BF16)
    hot_src_t = (rows8[0:1, :] == sublane).astype(F32).astype(BF16)
    hot_tgt = (columns[:, 1:2] == lane).astype(F32)
    hot_neg = (columns[:, 3:4] == lane).astype(F32)
    multiplicity = jnp.sum(hot_neg, axis=0, keepdims=True)
    rel = columns[:, 2:3]
    edge = lax.broadcasted_iota(jnp.int32, (ROWS, 1), 0)
    live = (edge < cnt_ref[...]).astype(F32)
    state8[...] = jnp.zeros_like(state8)
    state8[0:2, 0:WIDTH] = opstate_ref[...]
    op_sums = state8[...].T
    ops_copy.wait()
    ops_split = [split(ops[r]) for r in range(2)]

    left_copy.wait_recv()
    left_high, left_low = split(left[...])
    in_high, in_low = dot(hot_src, left_high).astype(BF16), dot(hot_src, left_low).astype(BF16)
    inputs = (in_high, in_low)
    mapped = jnp.where(rel < 0.5, dot3(inputs, ops_split[0]), dot3(inputs, ops_split[1]))
    inv_mapped = lax.rsqrt(jnp.sum(mapped * mapped, -1, keepdims=True) + 1e-06)
    unit_mapped = mapped * inv_mapped
    unit_split = split(unit_mapped)
    inputs_t = (in_high.astype(F32).T.astype(BF16), in_low.astype(F32).T.astype(BF16))

    right_copy.wait_recv()
    right_block = right[...]
    inv_right = lax.rsqrt(jnp.sum(right_block * right_block, -1, keepdims=True) + 1e-06)
    unit_right = right_block * inv_right
    right_split = split(unit_right)
    scores = dot3(unit_split, right_split, NT)
    positive = jnp.exp(jnp.sum(hot_tgt * scores, -1, keepdims=True))
    weights = multiplicity * jnp.exp(scores)
    norm = positive + jnp.sum(weights, -1, keepdims=True)
    scale = live / norm
    pull = weights * scale + hot_tgt * (positive * scale - live)
    pull_split = split(pull)
    d_unit = dot3(pull_split, right_split)
    d_mapped = inv_mapped * (d_unit - unit_mapped * jnp.sum(unit_mapped * d_unit, -1, keepdims=True))

    def operator_grad(kind):
        picked = jnp.where(rel == kind.astype(F32), d_mapped, 0.0)
        return dot3(inputs_t, split(picked))

    grad[0, 0:WIDTH, 0:WIDTH] = operator_grad(other)
    pair_copy = send(grad.at[0], sibling, core_send.at[0], core_recv.at[0], pair)
    own = operator_grad(mc)
    grad[1, 0:WIDTH, 0:WIDTH] = own
    pair_copy.wait_recv()
    total[...] = grad[1] + sibling[...]

    first = (("x", X0, XC, rx, 0), ("y", Y0, YC, ry, 3), ("z", Z0, ZC, rz, 10))
    copies1 = []
    for axis, start, rows, slots, base in first:
        for steps in range(1, size[axis]):
            to = (me[axis] + steps) % size[axis]
            chunk = total.at[pl.ds(pl.multiple_of(start + to * rows, 8), rows)]
            copies1.append(
                send(chunk, slots.at[steps - 1], s1.at[base + steps - 1], v1.at[base + steps - 1], along(axis, steps))
            )

    rstate_copy.wait_recv()
    lstate_copy.wait_recv()
    rows8[4:5, :] = lstate[...]
    rows8[5:6, :] = rstate[...]
    sums = rows8[...].T
    d_right_unit = dot3(split(pull.T), unit_split)
    d_right = inv_right * (
        d_right_unit - unit_right * jnp.sum(unit_right * d_right_unit, -1, keepdims=True)
    )
    out_right[...] = adagrad(right_block, sums[:, 5:6], d_right)
    right_out = pltpu.make_async_copy(out_right, new_right_ref, out_sem.at[0])
    right_out.start()
    d_inputs = dot3(split(jnp.where(rel < 0.5, d_mapped, 0.0)), ops_split[0], NT) + dot3(
        split(jnp.where(rel < 0.5, 0.0, d_mapped)), ops_split[1], NT
    )
    d_high, d_low = split(d_inputs)
    d_left = dot(hot_src_t, d_high) + dot(hot_src_t, d_low)
    out_left[...] = adagrad(left[...], sums[:, 4:5], d_left)
    left_out = pltpu.make_async_copy(out_left, new_left_ref, out_sem.at[1])
    left_out.start()

    def summed(start, rows, slots, count):
        value = total[pl.ds(pl.multiple_of(start, 8), rows), :]
        for slot in range(count):
            value = value + slots[slot]
        return value

    copies2 = []
    second = (("y", qx, r2x, 0), ("z", qy, r2y, 7), ("y", qz, r2z, 14))
    for part, (axis1, start, rows, slots, base1) in enumerate(first):
        axis, pieces, _, base = second[part]
        for steps in range(1, size[axis1]):
            copies1[base1 + steps - 1].wait_recv()
        value = summed(start + me[axis1] * rows, rows, slots, size[axis1] - 1)
        half = rows // 2
        for j in range(8):
            pieces[j] = value[half * (j // 4):half * (j // 4 + 1), 128 * (j % 4):128 * (j % 4 + 1)]
        for steps in range(1, size[axis]):
            to = (me[axis] + steps) % size[axis]
            k = base + steps - 1
            copies2.append(send(pieces.at[to], second[part][2].at[steps - 1], s2.at[k], v2.at[k], along(axis, steps)))

    third = (("z", r3x, 0), ("x", r3y, 7), ("x", r3z, 10))
    copies3 = []
    for part, (axis2, pieces, slots2, base2) in enumerate(second):
        axis, slots, base = third[part]
        for steps in range(1, size[axis2]):
            copies2[base2 + steps - 1].wait_recv()
        value = pieces[me[axis2]]
        for slot in range(size[axis2] - 1):
            value = value + slots2[slot]
        slots[me[axis]] = value
        for steps in range(1, size[axis]):
            k = base + steps - 1
            copies3.append(
                send(slots.at[me[axis]], slots.at[me[axis]], s3.at[k], v3.at[k], along(axis, steps))
            )

    finals = (fx, fy, fz)
    copies4 = []
    for part, (axis3, slots, base3) in enumerate(third):
        axis1, axis2 = first[part][0], second[part][0]
        base = second[part][3]
        for steps in range(1, size[axis3]):
            copies3[base3 + steps - 1].wait_recv()
        value = slots[0]
        for slot in range(1, size[axis3]):
            value = value + slots[slot]
        final = finals[part]
        final[mc, me[axis1], me[axis2]] = value
        for steps in range(1, size[axis2]):
            k = base + steps - 1
            piece = final.at[mc, me[axis1], me[axis2]]
            copies4.append(send(piece, piece, s4.at[k], v4.at[k], along(axis2, steps)))

    copies5, copies6 = [], []
    for part, (axis1, _, _, _, base1) in enumerate(first):
        axis2, base2 = second[part][0], second[part][3]
        final = finals[part]
        for steps in range(1, size[axis2]):
            copies4[base2 + steps - 1].wait_recv()
        chunk = final.at[mc, me[axis1]]
        for steps in range(1, size[axis1]):
            k = base1 + steps - 1
            copies5.append(send(chunk, chunk, s5.at[k], v5.at[k], along(axis1, steps)))
        copies6.append(send(chunk, chunk, s6.at[part], v6.at[part], pair))
    for part, (axis1, _, _, _, base1) in enumerate(first):
        final = finals[part]
        for steps in range(1, size[axis1]):
            k = base1 + steps - 1
            copies5[k].wait_recv()
            chunk = final.at[mc, (me[axis1] + size[axis1] - steps) % size[axis1]]
            copies6.append(send(chunk, chunk, s6.at[3 + k], v6.at[3 + k], pair))
    for copy in copies6:
        copy.wait_recv()

    for kind in range(2):
        for part, (axis1, start, rows, _, _) in enumerate(first):
            half = rows // 2
            for j in range(size[axis1]):
                for h in range(2):
                    row = start + j * rows + h * half
                    if row >= WIDTH:
                        continue
                    gradient = jnp.concatenate([finals[part][kind, j, 4 * h + q] for q in range(4)], axis=-1)
                    gradient = gradient[:, 0:WIDTH]
                    old = ops[kind, row:row + half, :]
                    out_ops[kind, row:row + half, :] = adagrad(old, op_sums[row:row + half, kind:kind + 1], gradient)
    ops_out = pltpu.make_async_copy(out_ops, new_ops_ref, out_sem.at[2])
    ops_out.start()
    for copy in [right_copy, left_copy, rstate_copy, lstate_copy, pair_copy]:
        copy.wait_send()
    for copy in copies1 + copies2 + copies3 + copies4 + copies5 + copies6:
        copy.wait_send()
    right_out.wait()
    left_out.wait()
    ops_out.wait()


def body(
    left_table, left_state, right_table, right_state, operators, operator_state,
    sources, targets, relations, negatives, counts,
):
    vmem, hbm = pl.BlockSpec(memory_space=pltpu.VMEM), pl.BlockSpec(memory_space=pl.ANY)
    dma = pltpu.SemaphoreType.DMA

    def buf(*shape):
        return pltpu.VMEM(shape, F32)

    block = jax.ShapeDtypeStruct((ROWS, WIDTH), F32)
    new_left, new_right, new_operators = pl.pallas_call(
        kernel,
        out_shape=(block, block, jax.ShapeDtypeStruct((2, WIDTH, WIDTH), F32)),
        in_specs=[hbm, vmem, hbm, vmem, hbm, vmem, vmem, vmem, vmem, vmem, vmem],
        out_specs=(hbm, hbm, hbm),
        scratch_shapes=[
            buf(ROWS, WIDTH), buf(ROWS, WIDTH), buf(1, ROWS), buf(1, ROWS), buf(2, WIDTH, WIDTH),
            buf(ROWS, WIDTH), buf(ROWS, WIDTH), buf(2, WIDTH, WIDTH), buf(8, ROWS), buf(8, LANES),
            buf(2, PADDED, LANES), buf(PADDED, LANES), buf(PADDED, LANES),
            buf(3, XC, LANES), buf(7, YC, LANES), buf(7, ZC, LANES),
            buf(8, XC // 2, 128), buf(8, YC // 2, 128), buf(8, ZC // 2, 128),
            buf(7, XC // 2, 128), buf(7, YC // 2, 128), buf(7, ZC // 2, 128),
            buf(8, XC // 2, 128), buf(4, YC // 2, 128), buf(4, ZC // 2, 128),
            buf(2, 4, 8, XC // 2, 128), buf(2, 8, 8, YC // 2, 128), buf(2, 8, 8, ZC // 2, 128),
            dma((4,)), dma((4,)), dma((1,)), dma((3,)),
            dma((1,)), dma((1,)), dma((17,)), dma((17,)), dma((21,)), dma((21,)),
            dma((13,)), dma((13,)), dma((21,)), dma((21,)), dma((17,)), dma((17,)),
            dma((20,)), dma((20,)),
        ],
        compiler_params=pltpu.CompilerParams(
            collective_id=0, has_side_effects=True, vmem_limit_bytes=48 * 2**20
        ),
        name="bucket_round",
    )(
        left_table.reshape(ROWS, WIDTH), left_state.reshape(1, ROWS),
        right_table.reshape(ROWS, WIDTH), right_state.reshape(1, ROWS),
        operators, operator_state,
        sources.reshape(1, ROWS), targets.reshape(1, ROWS),
        relations.reshape(1, ROWS), negatives.reshape(1, ROWS), counts,
    )
    return new_left[None, None], new_right[None, None], new_operators


def solution(mesh):
    edges = P("lhs", "rhs", None)
    blocks = P("lhs", "rhs", None, None)
    return jax.shard_map(
        body,
        mesh=mesh,
        in_specs=(blocks, edges, blocks, edges, P(), P(), edges, edges, edges, edges, P("lhs", "rhs")),
        out_specs=(blocks, blocks, P()),
        check_vma=False,
    )
```

time: 396 us -> 106 us (0.27)
  waiting for transfers between devices: 282 us -> 0 us
  Pallas kernels: 0 us -> 96.7 us
  other arithmetic: 29.7 us -> 0 us
  matrix products: 24.9 us -> 0 us
  local copies, waits for them, and re-layouts: 27 us -> 7.89 us
  between operations: 17.6 us -> 1.51 us
  starting transfers between devices: 13.1 us -> 0 us
    psum x1 -> x0, waiting for transfers between devices: 272 us -> none  [body(): summed = lax.psum(operator_grad, ('lhs', 'rhs'))]
    pallas_call x0 -> x1, Pallas kernels: none -> 96.7 us  [body(): pl.pallas_call(kernel, out_shape=(block, block, jax.ShapeDtypeStruct((2,...]
    dot_general x9 -> x0, matrix products: 24.9 us -> none  [the longest x3 12.8 us: map_edges(): jnp.einsum('nbw,nwv->nbv', shaped, picked, precision=lax.Precision.HIGHEST)]
    scatter-add x4 -> x0, other arithmetic: 18.2 us -> none  [the longest x1 7.18 us: map_edges(): picked = operators[firsts]]
    ppermute x4 -> x0, starting transfers between devices: 13 us -> none  [from_behind(): return lax.ppermute(value, axis, pairs)]
    gather x6 -> x0, local copies, waits for them, and re-layouts: 12.7 us -> none  [the longest x3 6.74 us: bucket_loss(): positive = jnp.sum(unit_mapped * unit_right[targets], -1)]
    ppermute x4 -> x0, waiting for transfers between devices: 10.4 us -> none  [from_behind(): return lax.ppermute(value, axis, pairs)]
    reduce_sum x8 -> x0, other arithmetic: 5.11 us -> none  [the longest x3 2.26 us: adagrad(): summed = sums_in + jnp.mean(gradient * gradient, -1)]
  transfers between devices with their start and end apart: 5 -> 0, of which waited for: 2 -> 0; matrix products, arithmetic and copies ran while one was open for 6% -> 0% of each run, Pallas kernels for 0% -> 0%
where the time goes in v1:
time: 106 us
  Pallas kernels  96.7 us (91%)
  local copies, waits for them, and re-layouts  7.89 us (7%)
  between operations  1.51 us (1%)
    pallas_call x1, Pallas kernels, body(): pl.pallas_call(kernel, out_shape=(block, block, jax.ShapeDtypeStruct((2,...  96.7 us
    unnamed x27, local copies, waits for them, and re-layouts  7.89 us

profile of v1, /device:TPU:1, one launch (start us, length us, event | category | flops | bytes accessed | tf_op | source)
XLA Modules:
  0.0 106.1 jit_solution(15275907817461870684)
XLA Ops:
  0.6 0.0 copy-start.9
  0.6 0.0 copy-start.8
  0.7 0.0 copy-start.7
  0.7 0.0 copy-start.6
  0.7 0.0 copy-start.3
  0.7 0.0 copy-start.5
  0.7 0.0 copy-start.10
  0.7 0.0 copy-start.4
  1.4 1.3 %copy.14 = f32[1,1,384,400]{3,2,1,0:T(8,128)S(1)} copy(f32[1,1,384,400]{2,3,1,0:T(8,128)} %param.11) | data formatting | bytes 1228800 | tf_op args[0]
  2.8 0.0 copy-done.10
  2.8 0.3 copy.15
  3.0 0.0 copy-done.9
  3.1 0.0 copy-done.8
  3.1 0.0 copy-done.7
  3.1 0.0 copy-done.6
  3.1 0.0 copy-done.3
  3.1 0.0 copy-done.5
  3.1 0.0 copy-done.4
  3.1 96.7 %bucket_round.1 = (f32[384,400]{1,0:T(8,128)S(1)}, f32[384,400]{1,0:T(8,128)S(1)}, f32[2,400,400]{2,1,0:T(8,128)S(1)}) custom-call(f32[384,400]{1,0:T(8,128)S(1)} %bitcast.10, f32[1,384]{1,0:T(1,128)S(1)} %bitcast.14, f32[384,400]{1,0:T(8,128)S(1)} %bitcast.11, f32[1,384]{1,0:T(1,128)S(1)} %bitcast.15, f32[2,400,400]{2,1,0:T(8,128)} %ops_ref.1, ...), custom_call_target="tpu_custom_call" | custom-call | tf_op jit(solution)/shard_map/bucket_round/pallas_call | solution.py:299
  99.9 0.0 copy-start
  99.9 0.9 copy-done
  100.8 0.0 copy-start.2
  100.8 0.9 copy-done.2
  101.6 0.0 copy-start.1
  101.6 2.3 %copy.16 = f32[1,1,384,400]{2,3,1,0:T(8,128)} copy(f32[1,1,384,400]{3,2,1,0:T(8,128)} %bitcast.13) | data formatting | bytes 1228800
  103.9 0.0 copy-done.1
  103.9 1.1 %copy.17 = f32[1,1,384,400]{2,3,1,0:T(8,128)} copy(f32[1,1,384,400]{3,2,1,0:T(8,128)S(1)} %bitcast.12) | data formatting | bytes 1228800
  105.0 1.2 %copy.20 = f32[2,400,400]{2,1,0:T(8,128)} copy(f32[2,400,400]{2,1,0:T(8,128)S(1)} %get-tuple-element.17) | data formatting | bytes 2560000
Async XLA Ops:
  0.6 2.4 %copy-start.9 = (s32[1,1,384]{2,1,0:T(1,128)S(1)}, s32[1,1,384]{2,1,0:T(1,128)}, u32[]{:S(2)}) copy-start(s32[1,1,384]{2,1,0:T(1,128)} %param.20) | copy-start | bytes 4612
  0.6 2.4 %copy-start.8 = (s32[1,1,384]{2,1,0:T(1,128)S(1)}, s32[1,1,384]{2,1,0:T(1,128)}, u32[]{:S(2)}) copy-start(s32[1,1,384]{2,1,0:T(1,128)} %param.19) | copy-start | bytes 4612
  0.7 2.4 %copy-start.7 = (s32[1,1,384]{2,1,0:T(1,128)S(1)}, s32[1,1,384]{2,1,0:T(1,128)}, u32[]{:S(2)}) copy-start(s32[1,1,384]{2,1,0:T(1,128)} %param.18) | copy-start | bytes 4612
  0.7 2.4 %copy-start.6 = (s32[1,1,384]{2,1,0:T(1,128)S(1)}, s32[1,1,384]{2,1,0:T(1,128)}, u32[]{:S(2)}) copy-start(s32[1,1,384]{2,1,0:T(1,128)} %param.17) | copy-start | bytes 4612
  0.7 2.4 %copy-start.3 = (f32[2,400]{1,0:T(2,128)S(1)}, f32[2,400]{1,0:T(2,128)}, u32[]{:S(2)}) copy-start(f32[2,400]{1,0:T(2,128)} %opstate_ref.1) | copy-start | bytes 9604
  0.7 2.4 %copy-start.5 = (f32[1,1,384]{2,1,0:T(1,128)S(1)}, f32[1,1,384]{2,1,0:T(1,128)}, u32[]{:S(2)}) copy-start(f32[1,1,384]{2,1,0:T(1,128)} %param.14) | copy-start | bytes 4612
  0.7 2.1 %copy-start.10 = (f32[1,1,384,400]{2,3,1,0:T(8,128)S(1)}, f32[1,1,384,400]{2,3,1,0:T(8,128)}, u32[]{:S(2)}) copy-start(f32[1,1,384,400]{2,3,1,0:T(8,128)} %param.13) | copy-start | bytes 1843204
  0.7 2.4 %copy-start.4 = (f32[1,1,384]{2,1,0:T(1,128)S(1)}, f32[1,1,384]{2,1,0:T(1,128)}, u32[]{:S(2)}) copy-start(f32[1,1,384]{2,1,0:T(1,128)} %param.12) | copy-start | bytes 4612
  99.9 0.9 copy-start
  100.8 0.9 copy-start.2
  101.6 2.3 %copy-start.1 = (f32[384,400]{1,0:T(8,128)S(1)}, f32[384,400]{1,0:T(8,128)}, u32[]{:S(2)}) copy-start(f32[384,400]{1,0:T(8,128)} %copy-done) | copy-start | bytes 1843204

commit v2 on v1

v2 whole, which is shorter than its diff:
```python
import functools

import jax
import jax.numpy as jnp
from jax import lax
from jax.experimental import pallas as pl
from jax.experimental.pallas import tpu as pltpu
from jax.sharding import PartitionSpec as P

MESH = pl.DeviceIdType.MESH
F32 = jnp.float32
BF16 = jnp.bfloat16

ROWS = 384
WIDTH = 400
VMEM_BYTES = 64 * 2**20 - 4096
NX, NY, NZ = 4, 8, 8
CUT = 208
PIECES = ((0, 104), (104, 104), (208, 96), (304, 96))

UNITS = 160
XC, YC, ZC = 20, 5, 5
X0, Y0, Z0 = 0, 80, 120

NN = (((1,), (0,)), ((), ()))
NT = (((1,), (1,)), ((), ()))


def split(value):
    high = value.astype(BF16)
    return high, (value - high.astype(F32)).astype(BF16)


def dot(a, b, dims=NN):
    return lax.dot_general(a, b, dims, preferred_element_type=F32)


def dot3(a, b, dims=NN):
    (a_high, a_low), (b_high, b_low) = a, b
    return dot(a_high, b_high, dims) + (dot(a_high, b_low, dims) + dot(a_low, b_high, dims))


def device(x, y, z, c):
    return ((z // 4) * 16 + y * 2 + c, (z % 4) * 4 + x)


def adagrad(weights, sums, gradient, axis):
    summed = sums + jnp.sum(gradient * gradient, axis, keepdims=True) * (1.0 / WIDTH)
    return weights - gradient * (0.1 / jnp.sqrt(summed))


def kernel(
    left_ref, lstate_ref, right_ref, rstate_ref, ops_ref, opstate_hbm,
    src_hbm, tgt_hbm, rel_hbm, neg_hbm, cnt_hbm,
    new_left_ref, new_right_ref, new_ops_ref,
    left, right, lstate, rstate, ops, out_left, out_right, out_ops, rows8, state8, tails, gsum,
    grad, sibling, total,
    rx, ry, rz, qx, qy, qz, r2x, r2y, r2z, r3x, r3y, r3z, fx, fy, fz,
    opstate_ref, src_ref, tgt_ref, rel_ref, neg_ref, cnt_ref,
    perm_send, perm_recv, local_sem, out_sem,
    core_send, core_recv, s1, v1, s2, v2, s3, v3, s4, v4, s5, v5, s6, v6,
):
    lhs, rhs = lax.axis_index("lhs"), lax.axis_index("rhs")
    mx, my, mz, mc = rhs % 4, (lhs // 2) % 8, (lhs // 16) * 4 + rhs // 4, lhs % 2
    other = 1 - mc

    def along(axis, steps):
        if axis == "x":
            return device((mx + steps) % NX, my, mz, mc)
        if axis == "y":
            return device(mx, (my + steps) % NY, mz, mc)
        return device(mx, my, (mz + steps) % NZ, mc)

    pair = device(mx, my, mz, other)
    size = {"x": NX, "y": NY, "z": NZ}
    me = {"x": mx, "y": my, "z": mz}

    peers = [((lhs + 1) % 32, rhs), ((lhs + 31) % 32, rhs), (lhs, (rhs + 1) % 16), (lhs, (rhs + 15) % 16)]
    peers += [pair, (lhs + 15 - 2 * (lhs % 16), rhs)]
    peers += [along(axis, steps) for axis in "xyz" for steps in range(1, size[axis])]
    barrier = pltpu.get_barrier_semaphore()
    for peer in peers:
        pl.semaphore_signal(barrier, inc=1, device_id=peer, device_id_type=MESH)
    place = lhs % 16
    for spot, steps in ((15, (14, 3)), (13, (18, 19)), (2, (29, 30)), (0, (13, 2))):
        @pl.when(place == spot)
        def _():
            for step in steps:
                pl.semaphore_signal(
                    barrier, inc=1, device_id=((lhs + step) % 32, rhs), device_id_type=MESH
                )
    greeted = len(peers) + 2 * ((place == 15) | (place == 13) | (place == 2) | (place == 0)).astype(jnp.int32)
    loads = [
        pltpu.make_async_copy(far, near, local_sem.at[i])
        for i, (far, near) in enumerate((
            (src_hbm, src_ref), (tgt_hbm, tgt_ref), (rel_hbm, rel_ref), (neg_hbm, neg_ref), (cnt_hbm, cnt_ref),
            (opstate_hbm, opstate_ref), (ops_ref, ops),
        ))
    ]
    for load in loads:
        load.start()
    pl.semaphore_wait(barrier, greeted)

    def make(src, dst, ssem, rsem, target):
        return pltpu.make_async_remote_copy(
            src_ref=src, dst_ref=dst, send_sem=ssem, recv_sem=rsem, device_id=target, device_id_type=MESH
        )

    def send(src, dst, ssem, rsem, target):
        copy = make(src, dst, ssem, rsem, target)
        copy.start()
        return copy

    parts = (pl.ds(0, CUT), pl.ds(CUT, WIDTH - CUT))
    corner_r, corner_l = (rhs % 4) == 3, (lhs % 16) == 15
    next_r, next_l = (rhs + 1) % 16, (lhs + 1) % 32
    hop_r = (jnp.where(corner_r, rhs - 3, next_r),) * 2 + (jnp.where(corner_r, (rhs + 4) % 16, next_r),) * 2
    hop_l = (
        next_l,
        jnp.where(corner_l, (lhs + 16) % 32, next_l),
        jnp.where(corner_l, (lhs + 14) % 32, next_l),
        jnp.where(corner_l, (lhs + 3) % 32, next_l),
    )
    slot_r = (corner_r.astype(jnp.int32),) * 4
    slot_l = (0,) + (corner_l.astype(jnp.int32),) * 3
    sent, got_r, got_l = [], {}, {}
    for p in (2, 0, 3, 1):
        part = pl.ds(*PIECES[p])
        sent.append(send(
            left_ref.at[part], left.at[slot_l[p], part],
            perm_send.at[4 + p], perm_recv.at[slot_l[p], 4 + p], (hop_l[p], rhs),
        ))
        sent.append(send(
            right_ref.at[part], right.at[slot_r[p], part],
            perm_send.at[p], perm_recv.at[slot_r[p], p], (lhs, hop_r[p]),
        ))
        got_r[p] = make(right.at[1, part], right.at[0, part], perm_send.at[10 + p], perm_recv.at[0, p], pair)
        got_l[p] = make(left.at[1, part], left.at[0, part], perm_send.at[14 + p], perm_recv.at[0, 4 + p], pair)
    rstate_copy = send(rstate_ref, rstate, perm_send.at[8], perm_recv.at[0, 8], (lhs, next_r))
    lstate_copy = send(lstate_ref, lstate, perm_send.at[9], perm_recv.at[0, 9], (next_l, rhs))
    sent += [rstate_copy, lstate_copy]

    def relay(here, buffer, p, base, target):
        part, sem = pl.ds(*PIECES[p]), perm_send.at[10 + base + p]

        @pl.when(here)
        def _():
            make(buffer.at[0, part], buffer.at[1, part], sem, perm_recv.at[1, base + p], pair).wait_recv()
            make(buffer.at[1, part], buffer.at[0, part], sem, perm_recv.at[0, base + p], target).start()

    def relayed(here, buffer, p, base):
        part, sem = pl.ds(*PIECES[p]), perm_send.at[10 + base + p]

        @pl.when(here)
        def _():
            make(buffer.at[1, part], buffer.at[0, part], sem, perm_recv.at[0, base + p], pair).wait_send()

    relays = [
        (corner_r, right, 2, 0, (lhs, rhs - 3)),
        ((rhs % 4) == 0, right, 0, 0, (lhs, (rhs + 4) % 16)),
        (corner_l, left, 1, 4, (lhs - 15, rhs)),
        ((lhs % 16) == 13, left, 2, 4, (lhs - 13, rhs)),
        ((lhs % 16) == 2, left, 3, 4, (lhs - 2, rhs)),
        (corner_r, right, 3, 0, (lhs, rhs - 3)),
        ((rhs % 4) == 0, right, 1, 0, (lhs, (rhs + 4) % 16)),
    ]

    for load in loads[:6]:
        load.wait()
    rows8[0:1, :] = src_ref[...].astype(F32)
    rows8[1:2, :] = tgt_ref[...].astype(F32)
    rows8[2:3, :] = rel_ref[...].astype(F32)
    rows8[3:4, :] = neg_ref[...].astype(F32)
    rows8[4:8, :] = jnp.zeros((4, ROWS), F32)
    columns = rows8[...].T
    lane = lax.broadcasted_iota(jnp.int32, (ROWS, ROWS), 1).astype(F32)
    sublane = lax.broadcasted_iota(jnp.int32, (ROWS, ROWS), 0).astype(F32)
    hot_src = (columns[:, 0:1] == lane).astype(F32).astype(BF16)
    hot_src_t = (rows8[0:1, :] == sublane).astype(F32).astype(BF16)
    hot_tgt = (columns[:, 1:2] == lane).astype(F32)
    hot_neg = (columns[:, 3:4] == lane).astype(F32)
    multiplicity = jnp.sum(hot_neg, axis=0, keepdims=True)
    rel = rows8[2:3, :]
    edge = lax.broadcasted_iota(jnp.int32, (ROWS, 1), 0)
    live = (edge < cnt_ref[...]).astype(F32)
    state8[...] = jnp.zeros_like(state8)
    state8[0:2, 0:WIDTH] = opstate_ref[...]
    op_sums = state8[...].T
    tails[...] = jnp.zeros_like(tails)
    spare = jnp.zeros((4, 8, 128), F32)
    qx[20:24] = spare
    qy[5:8] = spare[0:3]
    qz[5:8] = spare[0:3]
    grad[0, 158:160] = spare[0:2]
    grad[1, 158:160] = spare[0:2]
    loads[6].wait()
    ops_split = [split(ops[r]) for r in range(2)]
    ops_t = [split(ops[r].T) for r in range(2)]

    for entry in relays:
        relay(*entry)

    in_high, in_low = [], []
    for p, part in enumerate(parts):
        got_l[2 * p].wait_recv()
        got_l[2 * p + 1].wait_recv()
        high, low = split(left[0, part, :])
        in_high.append(dot(high, hot_src_t).astype(BF16))
        in_low.append(dot(low, hot_src_t).astype(BF16))
    inputs = (jnp.concatenate(in_high, axis=0), jnp.concatenate(in_low, axis=0))
    mapped = jnp.where(rel < 0.5, dot3(ops_t[0], inputs), dot3(ops_t[1], inputs))
    inv_mapped = lax.rsqrt(jnp.sum(mapped * mapped, 0, keepdims=True) + 1e-06)
    unit_mapped = mapped * inv_mapped
    unit_rows = [split(unit_mapped[0:CUT].T), split(unit_mapped[CUT:WIDTH].T)]

    scores, square, right_split = 0.0, 0.0, []
    for p, part in enumerate(parts):
        got_r[2 * p].wait_recv()
        got_r[2 * p + 1].wait_recv()
        value = right[0, part, :]
        square = square + jnp.sum(value * value, 0, keepdims=True)
        right_split.append(split(value))
        scores = scores + dot3(unit_rows[p], right_split[p])
    inv_right = lax.rsqrt(square + 1e-06)
    scores = scores * inv_right
    positive = jnp.exp(jnp.sum(hot_tgt * scores, -1, keepdims=True))
    weights = multiplicity * jnp.exp(scores)
    norm = positive + jnp.sum(weights, -1, keepdims=True)
    scale = live / norm
    pull = weights * scale + hot_tgt * (positive * scale - live)
    pull_split = split(pull * inv_right)
    d_unit = jnp.concatenate([dot3(right_split[p], pull_split, NT) for p in range(2)], axis=0)
    d_mapped = inv_mapped * (d_unit - unit_mapped * jnp.sum(unit_mapped * d_unit, 0, keepdims=True))

    def operator_grad(kind, slot):
        high, low = split(jnp.where(rel == kind.astype(F32), d_mapped, 0.0))
        main = dot3(inputs, (high[0:ROWS], low[0:ROWS]), NT)
        for j in range(3):
            grad[slot, 50 * j:50 * j + 50] = main[:, 128 * j:128 * j + 128].reshape(50, 8, 128)
        tails[:, 0:WIDTH] = dot3((high[ROWS:WIDTH], low[ROWS:WIDTH]), inputs, NT)
        for i in range(2):
            for j in range(4):
                grad[slot, 150 + 4 * i + j] = tails[8 * i:8 * i + 8, 128 * j:128 * j + 128]

    operator_grad(other, 0)
    first = (("x", X0, XC, rx, 0), ("y", Y0, YC, ry, 3), ("z", Z0, ZC, rz, 10))
    pair_copies = []
    for part, (axis, start, count, _, _) in enumerate(first):
        span = pl.ds(start, count * size[axis])
        pair_copies.append(send(grad.at[0, span], sibling.at[span], core_send.at[part], core_recv.at[part], pair))
    operator_grad(mc, 1)
    copies1 = []
    for part, (axis, start, count, slots, base) in enumerate(first):
        pair_copies[part].wait_recv()
        span = pl.ds(start, count * size[axis])
        total[span] = grad[1, span] + sibling[span]
        for steps in range(1, size[axis]):
            to = (me[axis] + steps) % size[axis]
            k = base + steps - 1
            chunk = total.at[pl.ds(start + to * count, count)]
            copies1.append(send(chunk, slots.at[steps - 1], s1.at[k], v1.at[k], along(axis, steps)))

    rstate_copy.wait_recv()
    lstate_copy.wait_recv()
    unit_right = right[0] * inv_right
    d_right_unit = dot3(split(unit_mapped), split(pull))
    d_right = inv_right * (
        d_right_unit - unit_right * jnp.sum(unit_right * d_right_unit, 0, keepdims=True)
    )
    out_right[...] = adagrad(right[0], rstate[...], d_right, 0)
    right_out = pltpu.make_async_copy(out_right, new_right_ref, out_sem.at[0])
    right_out.start()
    d_inputs = dot3(ops_split[0], split(jnp.where(rel < 0.5, d_mapped, 0.0))) + dot3(
        ops_split[1], split(jnp.where(rel < 0.5, 0.0, d_mapped))
    )
    d_high, d_low = split(d_inputs)
    d_left = dot(d_high, hot_src) + dot(d_low, hot_src)
    out_left[...] = adagrad(left[0], lstate[...], d_left, 0)
    left_out = pltpu.make_async_copy(out_left, new_left_ref, out_sem.at[1])
    left_out.start()

    second = (("y", qx, r2x, 0, 3), ("z", qy, r2y, 7, 1), ("y", qz, r2z, 14, 1))
    copies2 = []
    for part, (axis1, start, count, slots, base1) in enumerate(first):
        axis, pieces, slots2, base, many = second[part]
        for steps in range(1, size[axis1]):
            copies1[base1 + steps - 1].wait_recv()
        value = total[pl.ds(start + me[axis1] * count, count)]
        for slot in range(size[axis1] - 1):
            value = value + slots[slot]
        pieces[0:count] = value
        for steps in range(1, size[axis]):
            to = (me[axis] + steps) % size[axis]
            k = base + steps - 1
            piece = pieces.at[pl.ds(to * many, many)]
            copies2.append(send(piece, slots2.at[steps - 1], s2.at[k], v2.at[k], along(axis, steps)))

    third = (("z", r3x, 0), ("x", r3y, 7), ("x", r3z, 10))
    copies3 = []
    for part, (axis2, pieces, slots2, base2, many) in enumerate(second):
        axis, slots, base = third[part]
        for steps in range(1, size[axis2]):
            copies2[base2 + steps - 1].wait_recv()
        value = pieces[pl.ds(me[axis2] * many, many)]
        for slot in range(size[axis2] - 1):
            value = value + slots2[slot]
        slots[me[axis]] = value
        for steps in range(1, size[axis]):
            k = base + steps - 1
            slot = slots.at[me[axis]]
            copies3.append(send(slot, slot, s3.at[k], v3.at[k], along(axis, steps)))

    finals = (fx, fy, fz)
    copies4 = []
    for part, (axis3, slots, base3) in enumerate(third):
        axis1 = first[part][0]
        axis2, _, _, base, many = second[part]
        for steps in range(1, size[axis3]):
            copies3[base3 + steps - 1].wait_recv()
        value = slots[0]
        for slot in range(1, size[axis3]):
            value = value + slots[slot]
        place = pl.ds(me[axis2] * many, many)
        finals[part][mc, me[axis1], place] = value
        piece = finals[part].at[mc, me[axis1], place]
        for steps in range(1, size[axis2]):
            k = base + steps - 1
            copies4.append(send(piece, piece, s4.at[k], v4.at[k], along(axis2, steps)))

    copies5, copies6 = [], []
    for part, (axis1, _, count, _, base1) in enumerate(first):
        axis2, _, _, base2, _ = second[part]
        for steps in range(1, size[axis2]):
            copies4[base2 + steps - 1].wait_recv()
        chunk = finals[part].at[mc, me[axis1], pl.ds(0, count)]
        for steps in range(1, size[axis1]):
            k = base1 + steps - 1
            copies5.append(send(chunk, chunk, s5.at[k], v5.at[k], along(axis1, steps)))
        copies6.append(send(chunk, chunk, s6.at[part], v6.at[part], pair))
    for part, (axis1, _, count, _, base1) in enumerate(first):
        for steps in range(1, size[axis1]):
            k = base1 + steps - 1
            copies5[k].wait_recv()
            chunk = finals[part].at[mc, (me[axis1] + size[axis1] - steps) % size[axis1], pl.ds(0, count)]
            copies6.append(send(chunk, chunk, s6.at[3 + k], v6.at[3 + k], pair))
    ops_out = []
    for turn, kind in enumerate((mc, other)):
        if turn:
            for copy in copies6:
                copy.wait_recv()
        for part, (axis1, start, count, _, _) in enumerate(first):
            for j in range(size[axis1]):
                for i in range(count):
                    unit = start + j * count + i
                    if unit < 150:
                        row, column = 8 * (unit % 50), 128 * (unit // 50)
                        gsum[row:row + 8, column:column + 128] = finals[part][kind, j, i]
                    elif unit < 158:
                        row, column = 8 * ((unit - 150) // 4), 128 * ((unit - 150) % 4)
                        tails[row:row + 8, column:column + 128] = finals[part][kind, j, i]
        gsum[:, ROWS:WIDTH] = tails[...].T[0:WIDTH]
        sums = jnp.where(kind == 0, op_sums[0:WIDTH, 0:1], op_sums[0:WIDTH, 1:2])
        out_ops[kind] = adagrad(ops[kind], sums, gsum[...], 1)
        ops_out.append(pltpu.make_async_copy(out_ops.at[kind], new_ops_ref.at[kind], out_sem.at[2 + turn]))
        ops_out[turn].start()
    for here, buffer, p, base, _ in relays:
        relayed(here, buffer, p, base)
    for copy in sent + pair_copies + copies1 + copies2 + copies3 + copies4 + copies5 + copies6:
        copy.wait_send()
    right_out.wait()
    left_out.wait()
    ops_out[0].wait()
    ops_out[1].wait()


def hand_over(left_ref, right_ref, ops_ref, new_left_ref, new_right_ref, new_ops_ref, blocks, ops, sems):
    steps = []
    for i, (source, target) in enumerate(((left_ref, new_left_ref), (right_ref, new_right_ref))):
        for start in range(0, WIDTH, 200):
            part = pl.ds(start, 200)
            steps.append((source.at[part], blocks.at[i, part], target.at[part]))
    for kind in range(2):
        for start in range(0, WIDTH, 200):
            part = pl.ds(start, 200)
            steps.append((ops_ref.at[kind, part], ops.at[kind, part], new_ops_ref.at[kind, part]))
    loads = [pltpu.make_async_copy(a, b, sems.at[0, i]) for i, (a, b, _) in enumerate(steps)]
    stores = [pltpu.make_async_copy(b, c, sems.at[1, i]) for i, (_, b, c) in enumerate(steps)]
    for load in loads:
        load.start()
    for load, store in zip(loads, stores):
        load.wait()
        store.start()
    for store in stores:
        store.wait()


def body(
    left_table, left_state, right_table, right_state, operators, operator_state,
    sources, targets, relations, negatives, counts,
):
    hbm = pl.BlockSpec(memory_space=pl.ANY)
    dma = pltpu.SemaphoreType.DMA

    def buf(*shape):
        return pltpu.VMEM(shape, F32)

    def units(*shape):
        return pltpu.VMEM(shape + (8, 128), F32)

    block = jax.ShapeDtypeStruct((WIDTH, ROWS), F32)
    results = (block, block, jax.ShapeDtypeStruct((2, WIDTH, WIDTH), F32))
    trained = pl.pallas_call(
        kernel,
        out_shape=results,
        in_specs=[hbm] * 11,
        out_specs=(hbm, hbm, hbm),
        scratch_shapes=[
            buf(2, WIDTH, ROWS), buf(2, WIDTH, ROWS), buf(1, ROWS), buf(1, ROWS), buf(2, WIDTH, WIDTH),
            buf(WIDTH, ROWS), buf(WIDTH, ROWS), buf(2, WIDTH, WIDTH), buf(8, ROWS), buf(8, 512),
            buf(16, 512), buf(WIDTH, WIDTH),
            units(2, UNITS), units(UNITS), units(UNITS),
            units(3, XC), units(7, YC), units(7, ZC),
            units(24), units(8), units(8),
            units(7, 3), units(7, 1), units(7, 1),
            units(8, 3), units(4, 1), units(4, 1),
            units(2, 4, 24), units(2, 8, 8), units(2, 8, 8),
            buf(2, WIDTH), *[pltpu.VMEM((1, ROWS), jnp.int32)] * 4, pltpu.VMEM((1, 1), jnp.int32),
            dma((18,)), dma((2, 10)), dma((7,)), dma((4,)),
            dma((3,)), dma((3,)), dma((17,)), dma((17,)), dma((21,)), dma((21,)),
            dma((13,)), dma((13,)), dma((21,)), dma((21,)), dma((17,)), dma((17,)),
            dma((20,)), dma((20,)),
        ],
        compiler_params=pltpu.CompilerParams(
            collective_id=0, has_side_effects=True, vmem_limit_bytes=VMEM_BYTES
        ),
        name="bucket_round",
    )(
        left_table.reshape(ROWS, WIDTH).T, left_state.reshape(1, ROWS),
        right_table.reshape(ROWS, WIDTH).T, right_state.reshape(1, ROWS),
        operators, operator_state,
        sources.reshape(1, ROWS), targets.reshape(1, ROWS),
        relations.reshape(1, ROWS), negatives.reshape(1, ROWS), counts,
    )
    new_left, new_right, new_operators = pl.pallas_call(
        hand_over,
        out_shape=results,
        in_specs=[hbm] * 3,
        out_specs=(hbm, hbm, hbm),
        scratch_shapes=[buf(2, WIDTH, ROWS), buf(2, WIDTH, WIDTH), dma((2, 8))],
        compiler_params=pltpu.CompilerParams(vmem_limit_bytes=VMEM_BYTES),
        name="hand_over",
    )(*trained)
    return new_left.T[None, None], new_right.T[None, None], new_operators


def solution(mesh):
    edges = P("lhs", "rhs", None)
    blocks = P("lhs", "rhs", None, None)
    return jax.shard_map(
        body,
        mesh=mesh,
        in_specs=(blocks, edges, blocks, edges, P(), P(), edges, edges, edges, edges, P("lhs", "rhs")),
        out_specs=(blocks, blocks, P()),
        check_vma=False,
    )
```

time: 106 us -> 78 us (0.74)
  Pallas kernels: 96.7 us -> 76.6 us
  local copies, waits for them, and re-layouts: 7.89 us -> 0 us
    pallas_call x1 -> x2, Pallas kernels: 96.7 us -> 76.6 us  [the longest x1 73.9 us: body(): pl.pallas_call(kernel, out_shape=results, in_specs=[hbm] * 11, out_specs=...]
    unnamed x27 -> x0, local copies, waits for them, and re-layouts: 7.89 us -> none
where the time goes in v2:
time: 78 us; the launch traced here: 77.8 us
  Pallas kernels  76.6 us (98%)
  between operations  1.29 us (2%)
    pallas_call x1, Pallas kernels, body(): pl.pallas_call(kernel, out_shape=results, in_specs=[hbm] * 11, out_specs=...  73.9 us
    pallas_call x1, Pallas kernels, body(): pl.pallas_call(hand_over, out_shape=results, in_specs=[hbm] * 3, out_spec...  2.67 us

profile of v2, /device:TPU:1, one launch (start us, length us, event | category | flops | bytes accessed | tf_op | source)
XLA Modules:
  0.0 77.8 jit_solution(1754823809786338269)
XLA Ops:
  1.3 73.9 %bucket_round.1 = (f32[400,384]{1,0:T(8,128)}, f32[400,384]{1,0:T(8,128)}, f32[2,400,400]{2,1,0:T(8,128)}) custom-call(f32[400,384]{1,0:T(8,128)} %bitcast.18, f32[1,384]{1,0:T(1,128)} %bitcast.20, f32[400,384]{1,0:T(8,128)} %bitcast.19, f32[1,384]{1,0:T(1,128)} %bitcast.21, f32[2,400,400]{2,1,0:T(8,128)} %ops_ref.1, f32[2,400]{1,0:T(2,128)} %opstate_hbm.1, ...), custom_call_target="tpu_custom_call" | custom-call | tf_op jit(solution)/shard_map/bucket_round/pallas_call | solution.py:412
  75.2 2.7 %hand_over.1 = (f32[400,384]{1,0:T(8,128)}, f32[400,384]{1,0:T(8,128)}, f32[2,400,400]{2,1,0:T(8,128)}) custom-call(f32[400,384]{1,0:T(8,128)} %get-tuple-element.9.left_ref, f32[400,384]{1,0:T(8,128)} %get-tuple-element.10.right_ref, f32[2,400,400]{2,1,0:T(8,128)} %get-tuple-element.11.ops_ref), custom_call_target="tpu_custom_call" | custom-call | tf_op jit(solution)/shard_map/hand_over/pallas_call | solution.py:444

commit v3 on v2

--- a/solution.py
+++ b/solution.py
@@ -19,8 +19,8 @@
 PIECES = ((0, 104), (104, 104), (208, 96), (304, 96))
 
 UNITS = 160
-XC, YC, ZC = 20, 5, 5
-X0, Y0, Z0 = 0, 80, 120
+XC, YC, ZC = 16, 6, 6
+X0, Y0, Z0 = 0, 64, 112
 
 NN = (((1,), (0,)), ((), ()))
 NT = (((1,), (1,)), ((), ()))
@@ -74,6 +74,9 @@
     pair = device(mx, my, mz, other)
     size = {"x": NX, "y": NY, "z": NZ}
     me = {"x": mx, "y": my, "z": mz}
+
+    def far(axis):
+        return sorted(range(1, size[axis]), key=lambda d: -min(d, size[axis] - d))
 
     peers = [((lhs + 1) % 32, rhs), ((lhs + 31) % 32, rhs), (lhs, (rhs + 1) % 16), (lhs, (rhs + 15) % 16)]
     peers += [pair, (lhs + 15 - 2 * (lhs % 16), rhs)]
@@ -124,7 +127,7 @@
     slot_r = (corner_r.astype(jnp.int32),) * 4
     slot_l = (0,) + (corner_l.astype(jnp.int32),) * 3
     sent, got_r, got_l = [], {}, {}
-    for p in (2, 0, 3, 1):
+    for p in (0, 2, 1, 3):
         part = pl.ds(*PIECES[p])
         sent.append(send(
             left_ref.at[part], left.at[slot_l[p], part],
@@ -188,9 +191,8 @@
     op_sums = state8[...].T
     tails[...] = jnp.zeros_like(tails)
     spare = jnp.zeros((4, 8, 128), F32)
-    qx[20:24] = spare
-    qy[5:8] = spare[0:3]
-    qz[5:8] = spare[0:3]
+    qy[6:8] = spare[0:2]
+    qz[6:8] = spare[0:2]
     grad[0, 158:160] = spare[0:2]
     grad[1, 158:160] = spare[0:2]
     loads[6].wait()
@@ -249,16 +251,16 @@
         span = pl.ds(start, count * size[axis])
         pair_copies.append(send(grad.at[0, span], sibling.at[span], core_send.at[part], core_recv.at[part], pair))
     operator_grad(mc, 1)
-    copies1 = []
+    copies1 = {}
     for part, (axis, start, count, slots, base) in enumerate(first):
         pair_copies[part].wait_recv()
         span = pl.ds(start, count * size[axis])
         total[span] = grad[1, span] + sibling[span]
-        for steps in range(1, size[axis]):
+        for steps in far(axis):
             to = (me[axis] + steps) % size[axis]
             k = base + steps - 1
             chunk = total.at[pl.ds(start + to * count, count)]
-            copies1.append(send(chunk, slots.at[steps - 1], s1.at[k], v1.at[k], along(axis, steps)))
+            copies1[k] = send(chunk, slots.at[steps - 1], s1.at[k], v1.at[k], along(axis, steps))
 
     rstate_copy.wait_recv()
     lstate_copy.wait_recv()
@@ -279,8 +281,8 @@
     left_out = pltpu.make_async_copy(out_left, new_left_ref, out_sem.at[1])
     left_out.start()
 
-    second = (("y", qx, r2x, 0, 3), ("z", qy, r2y, 7, 1), ("y", qz, r2z, 14, 1))
-    copies2 = []
+    second = (("y", qx, r2x, 0, 2), ("x", qy, r2y, 7, 2), ("x", qz, r2z, 10, 2))
+    copies2, copies3, copies4, copies5, copies6 = {}, {}, {}, {}, {}
     for part, (axis1, start, count, slots, base1) in enumerate(first):
         axis, pieces, slots2, base, many = second[part]
         for steps in range(1, size[axis1]):
@@ -289,15 +291,15 @@
         for slot in range(size[axis1] - 1):
             value = value + slots[slot]
         pieces[0:count] = value
-        for steps in range(1, size[axis]):
+        for steps in far(axis):
             to = (me[axis] + steps) % size[axis]
             k = base + steps - 1
             piece = pieces.at[pl.ds(to * many, many)]
-            copies2.append(send(piece, slots2.at[steps - 1], s2.at[k], v2.at[k], along(axis, steps)))
-
-    third = (("z", r3x, 0), ("x", r3y, 7), ("x", r3z, 10))
-    copies3 = []
-    for part, (axis2, pieces, slots2, base2, many) in enumerate(second):
+            copies2[k] = send(piece, slots2.at[steps - 1], s2.at[k], v2.at[k], along(axis, steps))
+
+    third = (("z", r3x, 0), ("z", r3y, 7), ("y", r3z, 14))
+    for part in (0, 1, 2):
+        axis2, pieces, slots2, base2, many = second[part]
         axis, slots, base = third[part]
         for steps in range(1, size[axis2]):
             copies2[base2 + steps - 1].wait_recv()
@@ -305,14 +307,14 @@
         for slot in range(size[axis2] - 1):
             value = value + slots2[slot]
         slots[me[axis]] = value
-        for steps in range(1, size[axis]):
+        for steps in far(axis):
             k = base + steps - 1
             slot = slots.at[me[axis]]
-            copies3.append(send(slot, slot, s3.at[k], v3.at[k], along(axis, steps)))
+            copies3[k] = send(slot, slot, s3.at[k], v3.at[k], along(axis, steps))
 
     finals = (fx, fy, fz)
-    copies4 = []
-    for part, (axis3, slots, base3) in enumerate(third):
+    for part in (0, 1, 2):
+        axis3, slots, base3 = third[part]
         axis1 = first[part][0]
         axis2, _, _, base, many = second[part]
         for steps in range(1, size[axis3]):
@@ -323,30 +325,30 @@
         place = pl.ds(me[axis2] * many, many)
         finals[part][mc, me[axis1], place] = value
         piece = finals[part].at[mc, me[axis1], place]
-        for steps in range(1, size[axis2]):
+        for steps in far(axis2):
             k = base + steps - 1
-            copies4.append(send(piece, piece, s4.at[k], v4.at[k], along(axis2, steps)))
-
-    copies5, copies6 = [], []
-    for part, (axis1, _, count, _, base1) in enumerate(first):
+            copies4[k] = send(piece, piece, s4.at[k], v4.at[k], along(axis2, steps))
+
+    for part in (0, 1, 2):
+        axis1, _, count, _, base1 = first[part]
         axis2, _, _, base2, _ = second[part]
         for steps in range(1, size[axis2]):
             copies4[base2 + steps - 1].wait_recv()
         chunk = finals[part].at[mc, me[axis1], pl.ds(0, count)]
-        for steps in range(1, size[axis1]):
+        for steps in far(axis1):
             k = base1 + steps - 1
-            copies5.append(send(chunk, chunk, s5.at[k], v5.at[k], along(axis1, steps)))
-        copies6.append(send(chunk, chunk, s6.at[part], v6.at[part], pair))
+            copies5[k] = send(chunk, chunk, s5.at[k], v5.at[k], along(axis1, steps))
+        copies6[part] = send(chunk, chunk, s6.at[part], v6.at[part], pair)
     for part, (axis1, _, count, _, base1) in enumerate(first):
-        for steps in range(1, size[axis1]):
+        for steps in sorted(range(1, size[axis1]), key=lambda d: min(d, size[axis1] - d)):
             k = base1 + steps - 1
             copies5[k].wait_recv()
             chunk = finals[part].at[mc, (me[axis1] + size[axis1] - steps) % size[axis1], pl.ds(0, count)]
-            copies6.append(send(chunk, chunk, s6.at[3 + k], v6.at[3 + k], pair))
+            copies6[3 + k] = send(chunk, chunk, s6.at[3 + k], v6.at[3 + k], pair)
     ops_out = []
     for turn, kind in enumerate((mc, other)):
         if turn:
-            for copy in copies6:
+            for copy in copies6.values():
                 copy.wait_recv()
         for part, (axis1, start, count, _, _) in enumerate(first):
             for j in range(size[axis1]):
@@ -365,8 +367,11 @@
         ops_out[turn].start()
     for here, buffer, p, base, _ in relays:
         relayed(here, buffer, p, base)
-    for copy in sent + pair_copies + copies1 + copies2 + copies3 + copies4 + copies5 + copies6:
+    for copy in sent + pair_copies:
         copy.wait_send()
+    for copies in (copies1, copies2, copies3, copies4, copies5, copies6):
+        for copy in copies.values():
+            copy.wait_send()
     right_out.wait()
     left_out.wait()
     ops_out[0].wait()
@@ -420,14 +425,14 @@
             buf(16, 512), buf(WIDTH, WIDTH),
             units(2, UNITS), units(UNITS), units(UNITS),
             units(3, XC), units(7, YC), units(7, ZC),
-            units(24), units(8), units(8),
-            units(7, 3), units(7, 1), units(7, 1),
-            units(8, 3), units(4, 1), units(4, 1),
-            units(2, 4, 24), units(2, 8, 8), units(2, 8, 8),
+            units(XC), units(8), units(8),
+            units(7, 2), units(3, 2), units(3, 2),
+            units(8, 2), units(8, 2), units(8, 2),
+            units(2, 4, XC), units(2, 8, 8), units(2, 8, 8),
             buf(2, WIDTH), *[pltpu.VMEM((1, ROWS), jnp.int32)] * 4, pltpu.VMEM((1, 1), jnp.int32),
             dma((18,)), dma((2, 10)), dma((7,)), dma((4,)),
-            dma((3,)), dma((3,)), dma((17,)), dma((17,)), dma((21,)), dma((21,)),
-            dma((13,)), dma((13,)), dma((21,)), dma((21,)), dma((17,)), dma((17,)),
+            dma((3,)), dma((3,)), dma((17,)), dma((17,)), dma((13,)), dma((13,)),
+            dma((21,)), dma((21,)), dma((13,)), dma((13,)), dma((17,)), dma((17,)),
             dma((20,)), dma((20,)),
         ],
         compiler_params=pltpu.CompilerParams(

time: 78 us -> 71.3 us (0.914)
  Pallas kernels: 76.6 us -> 69.9 us
    pallas_call x1, Pallas kernels: 73.9 us -> 67.2 us  [body(): pl.pallas_call(kernel, out_shape=results, in_specs=[hbm] * 11, out_specs=...]
where the time goes in v3:
time: 71.3 us; the launch traced here: 71.1 us
  Pallas kernels  69.9 us (98%)
  between operations  1.29 us (2%)
    pallas_call x1, Pallas kernels, body(): pl.pallas_call(kernel, out_shape=results, in_specs=[hbm] * 11, out_specs=...  67.2 us
    pallas_call x1, Pallas kernels, body(): pl.pallas_call(hand_over, out_shape=results, in_specs=[hbm] * 3, out_spec...  2.67 us

profile of v3, /device:TPU:1, one launch (start us, length us, event | category | flops | bytes accessed | tf_op | source)
XLA Modules:
  0.0 71.1 jit_solution(14173403128702538190)
XLA Ops:
  1.3 67.2 %bucket_round.1 = (f32[400,384]{1,0:T(8,128)}, f32[400,384]{1,0:T(8,128)}, f32[2,400,400]{2,1,0:T(8,128)}) custom-call(f32[400,384]{1,0:T(8,128)} %bitcast.18, f32[1,384]{1,0:T(1,128)} %bitcast.20, f32[400,384]{1,0:T(8,128)} %bitcast.19, f32[1,384]{1,0:T(1,128)} %bitcast.21, f32[2,400,400]{2,1,0:T(8,128)} %ops_ref.1, f32[2,400]{1,0:T(2,128)} %opstate_hbm.1, ...), custom_call_target="tpu_custom_call" | custom-call | tf_op jit(solution)/shard_map/bucket_round/pallas_call | solution.py:417
  68.5 2.7 %hand_over.1 = (f32[400,384]{1,0:T(8,128)}, f32[400,384]{1,0:T(8,128)}, f32[2,400,400]{2,1,0:T(8,128)}) custom-call(f32[400,384]{1,0:T(8,128)} %get-tuple-element.9.left_ref, f32[400,384]{1,0:T(8,128)} %get-tuple-element.10.right_ref, f32[2,400,400]{2,1,0:T(8,128)} %get-tuple-element.11.ops_ref), custom_call_target="tpu_custom_call" | custom-call | tf_op jit(solution)/shard_map/hand_over/pallas_call | solution.py:449

commit v4 on v3

--- a/solution.py
+++ b/solution.py
@@ -347,10 +347,11 @@
             copies6[3 + k] = send(chunk, chunk, s6.at[3 + k], v6.at[3 + k], pair)
     ops_out = []
     for turn, kind in enumerate((mc, other)):
-        if turn:
-            for copy in copies6.values():
-                copy.wait_recv()
-        for part, (axis1, start, count, _, _) in enumerate(first):
+        for part, (axis1, start, count, _, base1) in enumerate(first):
+            if turn:
+                copies6[part].wait_recv()
+                for steps in range(1, size[axis1]):
+                    copies6[3 + base1 + steps - 1].wait_recv()
             for j in range(size[axis1]):
                 for i in range(count):
                     unit = start + j * count + i

time: 71.3 us -> 71.3 us (level)
  no operation moved by 1% of the time
where the time goes in v4:
time: 71.3 us; the launch traced here: 71.1 us
  Pallas kernels  69.9 us (98%)
  between operations  1.29 us (2%)
    pallas_call x1, Pallas kernels, body(): pl.pallas_call(kernel, out_shape=results, in_specs=[hbm] * 11, out_specs=...  67.2 us
    pallas_call x1, Pallas kernels, body(): pl.pallas_call(hand_over, out_shape=results, in_specs=[hbm] * 3, out_spec...  2.67 us

profile of v4, /device:TPU:1, one launch (start us, length us, event | category | flops | bytes accessed | tf_op | source)
XLA Modules:
  0.0 71.1 jit_solution(6722050212925350366)
XLA Ops:
  1.3 67.2 %bucket_round.1 = (f32[400,384]{1,0:T(8,128)}, f32[400,384]{1,0:T(8,128)}, f32[2,400,400]{2,1,0:T(8,128)}) custom-call(f32[400,384]{1,0:T(8,128)} %bitcast.18, f32[1,384]{1,0:T(1,128)} %bitcast.20, f32[400,384]{1,0:T(8,128)} %bitcast.19, f32[1,384]{1,0:T(1,128)} %bitcast.21, f32[2,400,400]{2,1,0:T(8,128)} %ops_ref.1, f32[2,400]{1,0:T(2,128)} %opstate_hbm.1, ...), custom_call_target="tpu_custom_call" | custom-call | tf_op jit(solution)/shard_map/bucket_round/pallas_call | solution.py:418
  68.5 2.7 %hand_over.1 = (f32[400,384]{1,0:T(8,128)}, f32[400,384]{1,0:T(8,128)}, f32[2,400,400]{2,1,0:T(8,128)}) custom-call(f32[400,384]{1,0:T(8,128)} %get-tuple-element.9.left_ref, f32[400,384]{1,0:T(8,128)} %get-tuple-element.10.right_ref, f32[2,400,400]{2,1,0:T(8,128)} %get-tuple-element.11.ops_ref), custom_call_target="tpu_custom_call" | custom-call | tf_op jit(solution)/shard_map/hand_over/pallas_call | solution.py:450
